TPU v7x, 32 devices: a whole 2x2x4 slice. The times are simulated.
32 devices in a mesh: grp: 2 (over x), tok: 16 (over z, y, core).
Axes of the slice: x: 2, y: 2, z: 4, core: 2. Of those that a mesh axis runs over, the one named last changes fastest.
Arguments:
- tokens: bfloat16 [4096, 2048], P(('grp', 'tok')), parts along dimension 0, may hold values from -6 to 6
- norm_gain: float32 [2048], replicated, may hold values from 0.1 to 1.9
- expert_ids: int32 [4096, 8], P(('grp', 'tok')), parts along dimension 0, may hold values from 0 to 15, as said below
- gate_weights: float32 [4096, 8], P(('grp', 'tok')), parts along dimension 0, may hold values from 0.05 to 1
- owner_map: int32 [16], replicated, may hold values from 0 to 15, each once
- in_q: bfloat16 [16, 2, 2048, 768], P('tok'), may hold values from -0.125 to 0.125
- in_scale: bfloat16 [16, 2, 768], P('tok'), may hold values from 0.5 to 2
- down_q: bfloat16 [16, 768, 2048], P('tok'), may hold values from -0.21875 to 0.21875
- down_scale: bfloat16 [16, 2048], P('tok'), may hold values from 0.5 to 2
Outputs:
- moe_out: bfloat16 [4096, 2048], P(('grp', 'tok')), parts along dimension 0
There are 2 independent parts, one for each index of `grp`. A program takes and returns all parts, laid end to end along the dimension named above; an argument that names none is the same for every part. Nothing has to cross between parts.
Inputs may be any that keep to these rules, and one draw needn't show every extreme that they name: `expert_ids`: each row names 8 different experts. One and the same expert is named by exactly 96 of the 128 rows of every device; every other expert is named by between 32 and 80 rows of each device, and 80 is reached on every device. `owner_map`: every slot holds exactly one expert.
All inputs are finite; a program needn't handle non-finite values.
Results may differ from a plain program's by a relative error of at most 0.0071.
Values may be sent and summed in bfloat16 or wider, within the bound.
A program may use at most 128 MiB of HBM per device.

v0:
```python
import jax
import jax.numpy as jnp
from jax import lax
from jax.sharding import PartitionSpec as P


def expert_rows(batch_rows, in_blocks, in_scales, down_block, down_scales):
    gate_part = jnp.dot(batch_rows, in_blocks[0], preferred_element_type=jnp.float32) * in_scales[0]
    up_part = jnp.dot(batch_rows, in_blocks[1], preferred_element_type=jnp.float32) * in_scales[1]
    hidden = (jax.nn.silu(gate_part) * up_part).astype(jnp.bfloat16)
    return (jnp.dot(hidden, down_block, preferred_element_type=jnp.float32) * down_scales).astype(
        jnp.bfloat16
    )


def on_device(
    tokens, norm_gain, expert_ids, gate_weights, owner_map, in_q, in_scale, down_q, down_scale
):
    tok_rows, model_width = tokens.shape
    top_count = expert_ids.shape[1]
    experts = owner_map.shape[0]
    mean_load = tok_rows * top_count // experts
    capacity = mean_load + mean_load // 2
    in_blocks = in_q[0]
    in_scales = in_scale[0]
    down_block = down_q[0]
    down_scales = down_scale[0]
    values = tokens.astype(jnp.float32)
    row_scale = lax.rsqrt(jnp.mean(values * values, axis=1, keepdims=True) + 1e-06)
    normed = (values * row_scale * norm_gain).astype(jnp.bfloat16)
    weights = gate_weights / jnp.sum(gate_weights, axis=1, keepdims=True)
    labels = jnp.arange(experts, dtype=jnp.int32)
    slot_table = jnp.sum(jnp.where(expert_ids[:, :, None] == labels, owner_map, 0), axis=2)
    flat_slot = slot_table.reshape(-1)
    onehot = (flat_slot[:, None] == labels).astype(jnp.int32)
    slot_rank = jnp.sum((jnp.cumsum(onehot, axis=0) - onehot) * onehot, axis=1)
    repeated = jnp.repeat(normed, top_count, axis=0)
    outgoing = (
        jnp.zeros((experts, capacity, model_width), jnp.bfloat16)
        .at[flat_slot, slot_rank]
        .set(repeated)
    )
    received = lax.all_to_all(outgoing, "tok", split_axis=0, concat_axis=0, tiled=True)
    source_count, slot_count, unused_width = received.shape
    flat_rows = received.reshape(source_count * slot_count, model_width)
    served = expert_rows(flat_rows, in_blocks, in_scales, down_block, down_scales)
    served = served.reshape(source_count, slot_count, model_width)
    returned_rows = lax.all_to_all(served, "tok", split_axis=0, concat_axis=0, tiled=True)
    picked = returned_rows[flat_slot, slot_rank].reshape(tok_rows, top_count, model_width)
    mixed = jnp.sum(weights[:, :, None] * picked.astype(jnp.float32), axis=1)
    return mixed.astype(jnp.bfloat16)


def solution(mesh):
    in_specs = (
        P(("grp", "tok"), None),
        P(),
        P(("grp", "tok"), None),
        P(("grp", "tok"), None),
        P(),
        P("tok", None, None, None),
        P("tok", None, None),
        P("tok", None, None),
        P("tok", None),
    )
    out_specs = P(("grp", "tok"), None)
    return jax.shard_map(
        on_device, mesh=mesh, in_specs=in_specs, out_specs=out_specs, check_vma=False
    )
```

profile of v0, /device:TPU:15, one launch (start us, length us, event | category | flops | bytes accessed | tf_op | source)
XLA Modules:
  0.0 365.0 jit_solution(7678618837900742371)
XLA Ops:
  0.0 0.0 copy-start
  0.0 0.9 select_reduce_fusion
  0.9 0.1 copy.19
  1.0 0.1 eq.45
  1.1 0.1 eq.41
  1.2 0.1 reshape.107
  1.3 4.5 %reduce-window.6 = s32[16,8,128]{2,1,0:T(8,128)S(1)} reduce-window(s32[16,8,128]{2,1,0:T(8,128)S(1)} %fusion.17, s32[]{:T(128)} %constant.10.clone.1), window={size=1x1x128 pad=0_0x0_0x127_0}, to_apply=%region_2.3 | reduce-window | flops 2080768 | bytes 131076 | tf_op jit(solution)/shard_map/reduce-window
  5.9 0.1 slice.30
  5.9 0.1 copy.22
  6.1 0.1 copy.23
  6.2 0.1 broadcast_add_fusion
  6.3 0.7 multiply_reduce_fusion
  7.1 0.8 and_reduce_fusion
  7.8 1.2 fusion.11
  9.1 2.0 fusion.13
  11.1 10.6 %scatter_custom_fusion = bf16[1536,2048]{1,0:T(8,128)(2,1)} fusion(s32[1024]{0:T(1024)S(1)} %broadcast_select_fusion, bf16[]{:T(256)} %constant.5.clone.1, bf16[128,2048]{1,0:T(8,128)(2,1)} %fusion.13), kind=kCustom, calls=%fused_computation.6 | custom fusion | bytes 6815746
  21.8 0.0 copy-start.3
  21.8 0.0 copy-start.2
  21.8 6.7 %all-to-all-start = ((bf16[16,96,2048]{2,1,0:T(8,128)(2,1)}), bf16[16,96,2048]{2,1,0:T(8,128)(2,1)}, u32[]{:S(2)}, u32[]{:S(2)}) async-start(bf16[16,96,2048]{2,1,0:T(8,128)(2,1)} %bitcast.43), calls=%async_computation | async-start | bytes 12582912 | tf_op jit(solution)/shard_map/all_to_all | solution.py:43
  28.4 0.0 copy-done.3
  28.5 0.0 copy-done.2
  28.5 137.3 %all-to-all-done = bf16[16,96,2048]{2,1,0:T(8,128)(2,1)} async-done(((bf16[16,96,2048]{2,1,0:T(8,128)(2,1)}), bf16[16,96,2048]{2,1,0:T(8,128)(2,1)}, u32[]{:S(2)}, u32[]{:S(2)}) %all-to-all-start) | async-done | bytes 6291488 | tf_op jit(solution)/shard_map/all_to_all | solution.py:43
  165.9 8.1 %fusion.5 = f32[1536,768]{1,0:T(8,128)S(1)} fusion(bf16[1536,2048]{1,0:T(8,128)(2,1)} %bitcast.5, bf16[1,2,2048,768]{3,2,1,0:T(8,128)(2,1)} %param.14), kind=kOutput, calls=%fused_computation.10 | convolution fusion | flops 4831838208 | bytes 14155776 | tf_op jit(solution)/shard_map/dot_general | solution.py:8
  173.9 8.6 %multiply_convert_fusion.1 = bf16[1536,768]{1,0:T(8,128)(2,1)S(1)} fusion(f32[1536,768]{1,0:T(8,128)S(1)} %fusion.5, bf16[1536,2048]{1,0:T(8,128)(2,1)} %bitcast.5, bf16[1,2,2048,768]{3,2,1,0:T(8,128)(2,1)} %param.14, f32[768]{0:T(1024)S(1)} %get-tuple-element.6, f32[768]{0:T(1024)S(1)} %get-tuple-element.5), kind=kOutput, calls=%fused_computation.5 | convolution fusion | flops 4841275392 | bytes 16521216 | tf_op jit(solution)/shard_map/dot_general | solution.py:9
  182.6 0.0 copy-done
  182.6 7.1 %multiply_convert_fusion = bf16[1536,2048]{1,0:T(8,128)(2,1)} fusion(bf16[1536,768]{1,0:T(8,128)(2,1)S(1)} %multiply_convert_fusion.1, f32[2048]{0:T(1024)S(1)} %bitcast.48, bf16[1,768,2048]{2,1,0:T(8,128)(2,1)S(1)} %copy-done), kind=kOutput, calls=%fused_computation.2 | convolution fusion | flops 4838129664 | bytes 11804672 | tf_op jit(solution)/shard_map/dot_general | solution.py:11
  189.7 0.0 copy-start.1
  189.7 5.0 %all-to-all-start.1 = ((bf16[16,96,2048]{2,1,0:T(8,128)(2,1)}), bf16[16,96,2048]{2,1,0:T(8,128)(2,1)}, u32[]{:S(2)}, u32[]{:S(2)}) async-start(bf16[16,96,2048]{2,1,0:T(8,128)(2,1)} %bitcast.44), calls=%async_computation.1 | async-start | bytes 12582912 | tf_op jit(solution)/shard_map/all_to_all | solution.py:48
  194.7 0.0 copy-done.1
  194.7 0.1 copy.18
  194.8 137.3 %all-to-all-done.1 = bf16[16,96,2048]{2,1,0:T(8,128)(2,1)} async-done(((bf16[16,96,2048]{2,1,0:T(8,128)(2,1)}), bf16[16,96,2048]{2,1,0:T(8,128)(2,1)}, u32[]{:S(2)}, u32[]{:S(2)}) %all-to-all-start.1) | async-done | bytes 6291488 | tf_op jit(solution)/shard_map/all_to_all | solution.py:48
  332.1 25.6 %gather_fusion = bf16[1024,2048]{1,0:T(8,128)(2,1)} fusion(bf16[16,96,2048]{2,1,0:T(8,128)(2,1)} %all-to-all-done.1, s32[1024]{0:T(1024)S(1)} %bitcast.42), kind=kCustom, calls=%fused_computation | custom fusion | bytes 8396800 | tf_op jit(solution)/shard_map/gather | solution.py:49
  357.7 7.3 %fusion = bf16[128,2048]{1,0:T(8,128)(2,1)} fusion(bf16[1024,2048]{1,0:T(8,128)(2,1)} %gather_fusion, f32[128,8]{1,0:T(8,128)S(1)} %copy.18), kind=kLoop, calls=%fused_computation.4 | loop fusion | flops 6029312 | bytes 4722688 | tf_op jit(solution)/shard_map/reduce_sum | solution.py:50
  (11 shorter events, 0.2 us)
Async XLA Ops:
  0.0 182.6 %copy-start = (bf16[1,768,2048]{2,1,0:T(8,128)(2,1)S(1)}, bf16[1,768,2048]{2,1,0:T(8,128)(2,1)}, u32[]{:S(2)}) copy-start(bf16[1,768,2048]{2,1,0:T(8,128)(2,1)} %param.16) | copy-start | bytes 9437188
  21.8 6.7 %copy-start.3 = (bf16[1,2048]{1,0:T(2,128)(2,1)S(1)}, bf16[1,2048]{1,0:T(2,128)(2,1)}, u32[]{:S(2)}) copy-start(bf16[1,2048]{1,0:T(2,128)(2,1)} %param.17) | copy-start | bytes 12292
  21.8 6.7 %copy-start.2 = (bf16[1,2,768]{2,1,0:T(2,128)(2,1)S(1)}, bf16[1,2,768]{2,1,0:T(2,128)(2,1)}, u32[]{:S(2)}) copy-start(bf16[1,2,768]{2,1,0:T(2,128)(2,1)} %param.15) | copy-start | bytes 9220
  21.8 144.1 %all-to-all-start = ((bf16[16,96,2048]{2,1,0:T(8,128)(2,1)}), bf16[16,96,2048]{2,1,0:T(8,128)(2,1)}, u32[]{:S(2)}, u32[]{:S(2)}) async-start(bf16[16,96,2048]{2,1,0:T(8,128)(2,1)} %bitcast.43), calls=%async_computation | async-start | bytes 12582912 | tf_op jit(solution)/shard_map/all_to_all | solution.py:43
  189.7 5.0 %copy-start.1 = (f32[128,8]{0,1:T(8,128)S(1)}, f32[128,8]{0,1:T(8,128)}, u32[]{:S(2)}) copy-start(f32[128,8]{0,1:T(8,128)} %param.12) | copy-start | bytes 12292
  189.7 142.5 %all-to-all-start.1 = ((bf16[16,96,2048]{2,1,0:T(8,128)(2,1)}), bf16[16,96,2048]{2,1,0:T(8,128)(2,1)}, u32[]{:S(2)}, u32[]{:S(2)}) async-start(bf16[16,96,2048]{2,1,0:T(8,128)(2,1)} %bitcast.44), calls=%async_computation.1 | async-start | bytes 12582912 | tf_op jit(solution)/shard_map/all_to_all | solution.py:48
where the time goes:
time: 366 us; the launch traced here: 365 us
  waiting for transfers between devices  275 us (75%)
  local copies, waits for them, and re-layouts  37 us (10%)
  matrix products  23.8 us (7%)
  other arithmetic  17.8 us (5%)
  starting transfers between devices  11.7 us (3%)
    all_to_all x1, waiting for transfers between devices, on_device(): lax.all_to_all(outgoing, 'tok', split_axis=0, concat_axis=0, tiled=True)  137 us
    all_to_all x1, waiting for transfers between devices, on_device(): lax.all_to_all(served, 'tok', split_axis=0, concat_axis=0, tiled=True)  137 us
    gather x1, local copies, waits for them, and re-layouts, on_device(): returned_rows[flat_slot, slot_rank]  25.6 us
    unnamed x9, local copies, waits for them, and re-layouts  10.7 us
    dot_general x1, matrix products, expert_rows(): jnp.dot(batch_rows, in_blocks[1], preferred_element_type=jnp.float32)  8.63 us
    dot_general x1, matrix products, expert_rows(): jnp.dot(batch_rows, in_blocks[0], preferred_element_type=jnp.float32)  8.07 us
    reduce_sum x1, other arithmetic, on_device(): mixed = jnp.sum(weights[:, :, None] * picked.astype(jnp.float32), axis=1)  7.33 us
  transfers between devices with their start and end apart: 2, of which 2 were waited for; matrix products, arithmetic and copies ran while one was open for 0% of the time, Pallas kernels for 0%

commit v1 on v0

--- a/solution.py
+++ b/solution.py
@@ -13,7 +13,13 @@
     )
 
 
-def on_device(
+def normalised(tokens, norm_gain):
+    values = tokens.astype(jnp.float32)
+    row_scale = lax.rsqrt(jnp.mean(values * values, axis=1, keepdims=True) + 1e-06)
+    return (values * row_scale * norm_gain).astype(jnp.bfloat16)
+
+
+def dispatched(
     tokens, norm_gain, expert_ids, gate_weights, owner_map, in_q, in_scale, down_q, down_scale
 ):
     tok_rows, model_width = tokens.shape
@@ -21,19 +27,16 @@
     experts = owner_map.shape[0]
     mean_load = tok_rows * top_count // experts
     capacity = mean_load + mean_load // 2
-    in_blocks = in_q[0]
-    in_scales = in_scale[0]
-    down_block = down_q[0]
-    down_scales = down_scale[0]
-    values = tokens.astype(jnp.float32)
-    row_scale = lax.rsqrt(jnp.mean(values * values, axis=1, keepdims=True) + 1e-06)
-    normed = (values * row_scale * norm_gain).astype(jnp.bfloat16)
+    normed = normalised(tokens, norm_gain)
     weights = gate_weights / jnp.sum(gate_weights, axis=1, keepdims=True)
     labels = jnp.arange(experts, dtype=jnp.int32)
     slot_table = jnp.sum(jnp.where(expert_ids[:, :, None] == labels, owner_map, 0), axis=2)
     flat_slot = slot_table.reshape(-1)
-    onehot = (flat_slot[:, None] == labels).astype(jnp.int32)
-    slot_rank = jnp.sum((jnp.cumsum(onehot, axis=0) - onehot) * onehot, axis=1)
+    onehot = (flat_slot[:, None] == labels).astype(jnp.bfloat16)
+    count = flat_slot.shape[0]
+    before = jnp.tri(count, count, -1, dtype=jnp.bfloat16)
+    ranks = jnp.dot(before, onehot, preferred_element_type=jnp.float32)
+    slot_rank = jnp.sum(ranks * onehot, axis=1).astype(jnp.int32)
     repeated = jnp.repeat(normed, top_count, axis=0)
     outgoing = (
         jnp.zeros((experts, capacity, model_width), jnp.bfloat16)
@@ -43,12 +46,33 @@
     received = lax.all_to_all(outgoing, "tok", split_axis=0, concat_axis=0, tiled=True)
     source_count, slot_count, unused_width = received.shape
     flat_rows = received.reshape(source_count * slot_count, model_width)
-    served = expert_rows(flat_rows, in_blocks, in_scales, down_block, down_scales)
+    served = expert_rows(flat_rows, in_q[0], in_scale[0], down_q[0], down_scale[0])
     served = served.reshape(source_count, slot_count, model_width)
     returned_rows = lax.all_to_all(served, "tok", split_axis=0, concat_axis=0, tiled=True)
     picked = returned_rows[flat_slot, slot_rank].reshape(tok_rows, top_count, model_width)
     mixed = jnp.sum(weights[:, :, None] * picked.astype(jnp.float32), axis=1)
     return mixed.astype(jnp.bfloat16)
+
+
+def gathered(
+    tokens, norm_gain, expert_ids, gate_weights, owner_map, in_q, in_scale, down_q, down_scale
+):
+    me = lax.axis_index("tok")
+    experts = owner_map.shape[0]
+    normed = normalised(tokens, norm_gain)
+    weights = gate_weights / jnp.sum(gate_weights, axis=1, keepdims=True)
+    labels = jnp.arange(experts, dtype=jnp.int32)
+    slot_table = jnp.sum(jnp.where(expert_ids[:, :, None] == labels, owner_map, 0), axis=2)
+    shares = jnp.sum(jnp.where(slot_table[:, :, None] == labels, weights[:, :, None], 0.0), axis=1)
+    all_rows = lax.all_gather(normed, "tok", axis=0, tiled=True)
+    all_shares = lax.all_gather(shares, "tok", axis=0, tiled=True)
+    share = jnp.sum(jnp.where(labels == me, all_shares, 0.0), axis=1, keepdims=True)
+    gate_part = jnp.dot(all_rows, in_q[0, 0], preferred_element_type=jnp.float32) * in_scale[0, 0]
+    up_part = jnp.dot(all_rows, in_q[0, 1], preferred_element_type=jnp.float32) * in_scale[0, 1]
+    hidden = (jax.nn.silu(gate_part) * up_part).astype(jnp.bfloat16)
+    served = jnp.dot(hidden, down_q[0], preferred_element_type=jnp.float32) * down_scale[0]
+    part = (served * share).astype(jnp.bfloat16)
+    return lax.psum_scatter(part, "tok", scatter_dimension=0, tiled=True)
 
 
 def solution(mesh):
@@ -64,6 +88,12 @@
         P("tok", None),
     )
     out_specs = P(("grp", "tok"), None)
+
+    def on_device(*args):
+        experts, top_count = args[4].shape[0], args[2].shape[1]
+        body = gathered if experts <= 2 * top_count else dispatched
+        return body(*args)
+
     return jax.shard_map(
         on_device, mesh=mesh, in_specs=in_specs, out_specs=out_specs, check_vma=False
     )

time: 366 us -> 231 us (0.63)
  the two profiles are of different devices: /device:TPU:15 before, /device:TPU:0 now
where the time goes in v1:
time: 231 us
  waiting for transfers between devices  154 us (67%)
  matrix products  32.4 us (14%)
  blocking collectives  23.9 us (10%)
  between operations  13.4 us (6%)
  other arithmetic  7.2 us (3%)
    reduce_scatter x1, waiting for transfers between devices, gathered(): return lax.psum_scatter(part, 'tok', scatter_dimension=0, tiled=True)  103 us
    all_gather x1, waiting for transfers between devices, gathered(): all_rows = lax.all_gather(normed, 'tok', axis=0, tiled=True)  50.4 us
    all_gather x1, blocking collectives, gathered(): all_shares = lax.all_gather(shares, 'tok', axis=0, tiled=True)  23.9 us
    dot_general x1, matrix products, gathered(): jnp.dot(hidden, down_q[0], preferred_element_type=jnp.float32)  20.7 us
    dot_general x1, matrix products, gathered(): jnp.dot(all_rows, in_q[0, 0], preferred_element_type=jnp.float32)  11.7 us
  transfers between devices with their start and end apart: 2, of which 2 were waited for; matrix products, arithmetic and copies ran while one was open for 2% of the time, Pallas kernels for 0%

profile of v1, /device:TPU:0, one launch (start us, length us, event | category | flops | bytes accessed | tf_op | source)
XLA Modules:
  0.0 230.5 jit_solution(16086576632089864007)
XLA Ops:
  6.5 0.0 copy-start
  6.5 0.0 all-gather.2.cloned.1.call-start
  6.5 1.4 fusion.11
  7.9 2.0 fusion.13
  10.0 0.0 all-gather.2.cloned.1.call-update
  10.0 0.0 reduce-scatter.2.cloned.1.call-start
  10.0 0.7 mul.80
  10.7 0.7 reduce_sum.47
  11.5 0.8 select_reduce_fusion.2
  12.2 0.7 broadcast_divide_fusion
  13.0 23.9 %all_gather.7 = f32[2048,16]{0,1:T(8,128)S(1)} all-gather(f32[128,16]{0,1:T(8,128)S(1)} %select_reduce_fusion.1), channel_id=1, replica_groups=mesh['grp'=2,'tok'=16] {'tok'}, dimensions={0}, use_global_device_ids=true | all-gather | bytes 139264 | tf_op jit(solution)/shard_map/all_gather | solution.py:68
  36.9 0.8 convert_reduce_fusion.1
  37.7 0.1 select_reduce_fusion
  37.8 50.4 %all-gather.2.cloned.1.call-done = bf16[2048,2048]{1,0:T(8,128)(2,1)} async-done(((bf16[128,2048]{1,0:T(8,128)(2,1)}), bf16[2048,2048]{1,0:T(8,128)(2,1)}) %all-gather.2.cloned.1.call-update) | async-done | bytes 8388624 | tf_op jit(solution)/shard_map/all_gather | solution.py:67
  88.2 11.7 %fusion.3 = f32[2048,768]{1,0:T(8,128)} fusion(bf16[2048,2048]{1,0:T(8,128)(2,1)} %all-gather.2.cloned.1.call-done, bf16[1,2,2048,768]{3,2,1,0:T(8,128)(2,1)} %param.14), kind=kOutput, calls=%fused_computation.4 | convolution fusion | flops 6442450944 | bytes 17825792 | tf_op jit(solution)/shard_map/dot_general | solution.py:70
  99.9 0.0 copy-done
  99.9 20.7 %multiply_convert_fusion = bf16[2048,2048]{1,0:T(8,128)(2,1)} fusion(f32[2048]{0:T(1024)S(1)} %select_reduce_fusion, f32[2048]{0:T(1024)S(1)} %bitcast.13, f32[2048,768]{1,0:T(8,128)} %fusion.3, bf16[2048,2048]{1,0:T(8,128)(2,1)} %all-gather.2.cloned.1.call-done, bf16[1,768,2048]{2,1,0:T(8,128)(2,1)S(1)} %copy-done, f32[768]{0:T(1024)S(1)} %get-tuple-element.6, ...), kind=kOutput, calls=%fused_computation | convolution fusion | flops 12910067712 | bytes 29382656 | tf_op jit(solution)/shard_map/dot_general | solution.py:73
  120.5 0.0 reduce-scatter.2.cloned.1.call-update
  120.6 103.1 %reduce-scatter.2.cloned.1.call-done = bf16[128,2048]{1,0:T(8,128)(2,1)} async-done(((bf16[2048,2048]{1,0:T(8,128)(2,1)}), bf16[128,2048]{1,0:T(8,128)(2,1)}) %reduce-scatter.2.cloned.1.call-update) | async-done | bytes 524304 | tf_op jit(solution)/shard_map/reduce_scatter | solution.py:75
  (3 shorter events, 0.0 us)
Async XLA Ops:
  6.5 93.3 %copy-start = (bf16[1,768,2048]{2,1,0:T(8,128)(2,1)S(1)}, bf16[1,768,2048]{2,1,0:T(8,128)(2,1)}, u32[]{:S(2)}) copy-start(bf16[1,768,2048]{2,1,0:T(8,128)(2,1)} %param.16) | copy-start | bytes 9437188
  6.5 81.6 %all-gather.2.cloned.1.call-start = ((), (), s32[]{:S(2)}) async-start(), calls=%async_computation.1 | async-start | bytes 8912896 | tf_op jit(solution)/shard_map/all_gather | solution.py:67
  10.0 213.7 %reduce-scatter.2.cloned.1.call-start = ((), (), s32[]{:S(2)}) async-start(), calls=%async_computation.2 | async-start | bytes 8912896 | tf_op jit(solution)/shard_map/reduce_scatter | solution.py:75
Sparse Core Ops, SparseCore 0:
  10.1 78.0 all-gather.1
  120.7 102.9 reduce-scatter.1

commit v2 on v1

--- a/solution.py
+++ b/solution.py
@@ -1,6 +1,10 @@
+import functools
+
 import jax
 import jax.numpy as jnp
 from jax import lax
+from jax.experimental import pallas as pl
+from jax.experimental.pallas import tpu as pltpu
 from jax.sharding import PartitionSpec as P
 
 
@@ -54,25 +58,218 @@
     return mixed.astype(jnp.bfloat16)
 
 
+def ring_kernel(
+    chips, experts, x_ref, in_ref, in_scale_ref, down_ref, down_scale_ref, out_ref,
+    rows, part, sib_in, ring_out, ring_in,
+    right_send, right_recv, left_send, left_recv, sib_send, sib_recv,
+    give_send, give_recv, sum_send, sum_recv,
+):
+    depth = chips // 2
+    model = out_ref.shape[1]
+    half = model // 2
+    me = lax.axis_index("tok")
+    core = lax.rem(me, 2)
+    chip = me // 2
+    place = chip // 2 + lax.rem(chip, 2) * (2 * depth - 1 - 2 * (chip // 2))
+
+    def chip_at(position):
+        position = lax.rem(position + 2 * chips, chips)
+        back = position // depth
+        return 2 * (position + back * (2 * depth - 1 - 2 * position)) + back
+
+    right = 2 * chip_at(place + 1) + core
+    left = 2 * chip_at(place - 1) + core
+    sibling = 2 * chip + 1 - core
+
+    def remote(src, dst, send, recv, target):
+        return pltpu.make_async_remote_copy(
+            src_ref=src, dst_ref=dst, send_sem=send, recv_sem=recv,
+            device_id={"tok": target}, device_id_type=pl.DeviceIdType.MESH,
+        )
+
+    def row_copy(position, side, send, recv, target):
+        block = rows.at[chip_at(position), side]
+        return remote(block, block, send, recv, target)
+
+    def go_right(k, position):
+        return row_copy(position, core, right_send.at[k], right_recv.at[k], right)
+
+    def go_left(k, position):
+        return row_copy(position, core, left_send.at[k], left_recv.at[k], left)
+
+    def share(offset, side):
+        return row_copy(place + offset, side, sib_send.at[offset], sib_recv.at[offset], sibling)
+
+    def give(offset):
+        block = chip_at(place + offset)
+        return remote(
+            part.at[block, 1 - core], sib_in.at[block], give_send.at[offset], give_recv.at[offset], sibling
+        )
+
+    rows[chip, core] = x_ref[...]
+    barrier = pltpu.get_barrier_semaphore()
+    for target in (left, right, sibling):
+        pl.semaphore_signal(
+            barrier, inc=1, device_id={"tok": target}, device_id_type=pl.DeviceIdType.MESH
+        )
+    pl.semaphore_wait(barrier, 3)
+
+    far_right, far_left = chips // 2, chips - 1 - chips // 2
+    go_right(0, place).start()
+    go_left(0, place).start()
+    share(0, core).start()
+
+    def gather_step(k, carry):
+        back = lax.rem(chips - k, chips)
+
+        @pl.when(k >= 1)
+        def _():
+            go_right(k - 1, place - k).wait_recv()
+
+            @pl.when(k < far_right)
+            def _():
+                go_right(k, place - k).start()
+
+            share(back, core).start()
+
+        @pl.when((k >= 1) & (k <= far_left))
+        def _():
+            go_left(k - 1, place + k).wait_recv()
+
+            @pl.when(k < far_left)
+            def _():
+                go_left(k, place + k).start()
+
+            share(k, core).start()
+
+        sides = jnp.where((k >= 1) & (k <= far_left), 2, 1)
+
+        def serve(turn, inner):
+            offset = jnp.where(turn == 0, back, k)
+            share(offset, 1 - core).wait_recv()
+            block = chip_at(place + offset)
+            batch = rows[block].reshape(-1, rows.shape[3])
+            lanes = batch[:, model:].astype(jnp.float32)
+            lane = lax.broadcasted_iota(jnp.int32, lanes.shape, 1)
+            chosen = (lane == me) | (lane == me + experts) | (lane == me + 2 * experts)
+            weight = jnp.sum(jnp.where(chosen, lanes, 0.0), axis=1, keepdims=True)
+            values = batch[:, :model]
+            gate = jnp.dot(values, in_ref[0], preferred_element_type=jnp.float32)
+            gate = gate * in_scale_ref[0:1, :].astype(jnp.float32)
+            up = jnp.dot(values, in_ref[1], preferred_element_type=jnp.float32)
+            up = up * in_scale_ref[1:2, :].astype(jnp.float32)
+            hidden = (gate / (1.0 + jnp.exp(-gate)) * up).astype(jnp.bfloat16)
+            wide = model // 4
+            for piece in range(4):
+                cut = slice(piece * wide, (piece + 1) * wide)
+                served = jnp.dot(hidden, down_ref[:, cut], preferred_element_type=jnp.float32)
+                served = served * down_scale_ref[:, cut].astype(jnp.float32) * weight
+                part[block, :, :, cut] = served.astype(jnp.bfloat16).reshape(2, -1, wide)
+            give(offset).start()
+            return inner
+
+        return lax.fori_loop(0, sides, serve, carry)
+
+    lax.fori_loop(0, far_right + 1, gather_step, 0)
+
+    def sum_copy(way, step):
+        target = right if way == 0 else left
+        return remote(
+            ring_out.at[way, step], ring_in.at[way, step],
+            sum_send.at[way, step], sum_recv.at[way, step], target,
+        )
+
+    def own(offset, way):
+        block = chip_at(place + offset)
+        cut = slice(way * half, (way + 1) * half)
+        return part[block, core, :, cut].astype(jnp.float32) + sib_in[block, :, cut].astype(jnp.float32)
+
+    def take(offset, carry):
+        give(offset).wait()
+        return carry
+
+    lax.fori_loop(0, chips, take, 0)
+    for way, first in ((0, chips - 1), (1, 1)):
+        ring_out[way, 0] = own(first, way).astype(jnp.bfloat16)
+        sum_copy(way, 0).start()
+
+    def sum_step(step, carry):
+        for way in range(2):
+            offset = chips - 1 - step if way == 0 else 1 + step
+            mine = own(offset, way)
+            sum_copy(way, step - 1).wait_recv()
+            ring_out[way, step] = (mine + ring_in[way, step - 1].astype(jnp.float32)).astype(jnp.bfloat16)
+            sum_copy(way, step).start()
+        return carry
+
+    lax.fori_loop(1, chips - 1, sum_step, 0)
+    for way in range(2):
+        mine = own(0, way)
+        sum_copy(way, chips - 2).wait_recv()
+        total = mine + ring_in[way, chips - 2].astype(jnp.float32)
+        out_ref[:, way * half : (way + 1) * half] = total.astype(jnp.bfloat16)
+
+    def ended(step, carry):
+        sum_copy(0, step).wait_send()
+        sum_copy(1, step).wait_send()
+        return carry
+
+    lax.fori_loop(0, chips - 1, ended, 0)
+
+    def shared(offset, carry):
+        share(offset, core).wait_send()
+        return carry
+
+    lax.fori_loop(0, chips, shared, 0)
+    for k in range(far_right):
+        go_right(k, place - k).wait_send()
+    for k in range(far_left):
+        go_left(k, place + k).wait_send()
+
+
 def gathered(
     tokens, norm_gain, expert_ids, gate_weights, owner_map, in_q, in_scale, down_q, down_scale
 ):
-    me = lax.axis_index("tok")
     experts = owner_map.shape[0]
+    tok_rows, model = tokens.shape
+    chips = experts // 2
     normed = normalised(tokens, norm_gain)
     weights = gate_weights / jnp.sum(gate_weights, axis=1, keepdims=True)
     labels = jnp.arange(experts, dtype=jnp.int32)
     slot_table = jnp.sum(jnp.where(expert_ids[:, :, None] == labels, owner_map, 0), axis=2)
     shares = jnp.sum(jnp.where(slot_table[:, :, None] == labels, weights[:, :, None], 0.0), axis=1)
-    all_rows = lax.all_gather(normed, "tok", axis=0, tiled=True)
-    all_shares = lax.all_gather(shares, "tok", axis=0, tiled=True)
-    share = jnp.sum(jnp.where(labels == me, all_shares, 0.0), axis=1, keepdims=True)
-    gate_part = jnp.dot(all_rows, in_q[0, 0], preferred_element_type=jnp.float32) * in_scale[0, 0]
-    up_part = jnp.dot(all_rows, in_q[0, 1], preferred_element_type=jnp.float32) * in_scale[0, 1]
-    hidden = (jax.nn.silu(gate_part) * up_part).astype(jnp.bfloat16)
-    served = jnp.dot(hidden, down_q[0], preferred_element_type=jnp.float32) * down_scale[0]
-    part = (served * share).astype(jnp.bfloat16)
-    return lax.psum_scatter(part, "tok", scatter_dimension=0, tiled=True)
+    high = lax.reduce_precision(shares, 8, 7)
+    middle = lax.reduce_precision(shares - high, 8, 7)
+    low = shares - high - middle
+    lanes = jnp.concatenate([high, middle, low], axis=1).astype(jnp.bfloat16)
+    pad = -lanes.shape[1] % 128
+    rows = jnp.concatenate([normed, jnp.pad(lanes, ((0, 0), (0, pad)))], axis=1)
+    width = rows.shape[1]
+    vmem = pl.BlockSpec(memory_space=pltpu.VMEM)
+    dma = pltpu.SemaphoreType.DMA
+    total_rows = 2 * chips * tok_rows
+    half = model // 2
+    return pl.pallas_call(
+        functools.partial(ring_kernel, chips, experts),
+        out_shape=jax.ShapeDtypeStruct((tok_rows, model), jnp.bfloat16),
+        in_specs=[vmem] * 5,
+        out_specs=vmem,
+        scratch_shapes=[
+            pltpu.VMEM((chips, 2, tok_rows, width), jnp.bfloat16),
+            pltpu.VMEM((chips, 2, tok_rows, model), jnp.bfloat16),
+            pltpu.VMEM((chips, tok_rows, model), jnp.bfloat16),
+            pltpu.VMEM((2, chips - 1, tok_rows, half), jnp.bfloat16),
+            pltpu.VMEM((2, chips - 1, tok_rows, half), jnp.bfloat16),
+            dma((chips,)), dma((chips,)), dma((chips,)), dma((chips,)), dma((chips,)), dma((chips,)),
+            dma((chips,)), dma((chips,)), dma((2, chips - 1)), dma((2, chips - 1)),
+        ],
+        compiler_params=pltpu.CompilerParams(
+            collective_id=0, has_side_effects=True, vmem_limit_bytes=60 * 1024 * 1024
+        ),
+        cost_estimate=pl.CostEstimate(
+            flops=6 * total_rows * model * in_q.shape[3], bytes_accessed=4 * total_rows * model, transcendentals=0
+        ),
+    )(rows, in_q[0], in_scale[0], down_q[0], down_scale)
 
 
 def solution(mesh):
@@ -91,7 +288,7 @@
 
     def on_device(*args):
         experts, top_count = args[4].shape[0], args[2].shape[1]
-        body = gathered if experts <= 2 * top_count else dispatched
+        body = gathered if experts <= 2 * top_count and experts % 4 == 0 else dispatched
         return body(*args)
 
     return jax.shard_map(

time: 231 us -> 122 us (0.53)
  waiting for transfers between devices: 154 us -> 0 us
  Pallas kernels: 0 us -> 114 us
  matrix products: 32.4 us -> 0 us
  blocking collectives: 23.9 us -> 0 us
  between operations: 13.4 us -> 0.04 us
    pallas_call x0 -> x1, Pallas kernels: none -> 114 us  [gathered(): pl.pallas_call(functools.partial(ring_kernel, chips, experts), out_shape=...]
    reduce_scatter x1 -> x0, waiting for transfers between devices: 103 us -> none  [gathered(): return lax.psum_scatter(part, 'tok', scatter_dimension=0, tiled=True)]
    all_gather x1 -> x0, waiting for transfers between devices: 50.4 us -> none  [gathered(): all_rows = lax.all_gather(normed, 'tok', axis=0, tiled=True)]
    dot_general x2 -> x0, matrix products: 32.4 us -> none  [the longest x1 20.7 us: gathered(): jnp.dot(hidden, down_q[0], preferred_element_type=jnp.float32)]
    all_gather x1 -> x0, blocking collectives: 23.9 us -> none  [gathered(): all_shares = lax.all_gather(shares, 'tok', axis=0, tiled=True)]
  transfers between devices with their start and end apart: 2 -> 0, of which waited for: 2 -> 0; matrix products, arithmetic and copies ran while one was open for 2% -> 0% of each run, Pallas kernels for 0% -> 0%
where the time goes in v2:
time: 122 us
  Pallas kernels  114 us (93%)
  other arithmetic  5.53 us (5%)
  local copies, waits for them, and re-layouts  2 us (2%)
    pallas_call x1, Pallas kernels, gathered(): pl.pallas_call(functools.partial(ring_kernel, chips, experts), out_shape=...  114 us

profile of v2, /device:TPU:0, one launch (start us, length us, event | category | flops | bytes accessed | tf_op | source)
XLA Modules:
  0.0 121.6 jit_solution(2069104735289761424)
XLA Ops:
  0.0 1.2 %fusion.1 = f32[128]{0:T(128)S(1)} fusion(bf16[128,2048]{1,0:T(8,128)(2,1)} %param.9), kind=kLoop, calls=%fused_computation.4 | loop fusion | flops 786304 | bytes 524800 | tf_op jit(solution)/shard_map/reduce_sum | solution.py:22
  1.2 0.7 reduce_sum.38
  1.9 0.7 broadcast_divide_fusion
  2.6 0.8 select_reduce_fusion.1
  3.5 0.1 copy.15
  3.6 1.2 %fusion.3 = bf16[128,2048]{1,0:T(8,128)(2,1)S(1)} fusion(bf16[128,2048]{1,0:T(8,128)(2,1)} %param.9, f32[2048]{0:T(1024)} %param.10, f32[128]{0:T(128)S(1)} %add_rsqrt_fusion), kind=kLoop, calls=%fused_computation.6 | loop fusion | flops 1048576 | bytes 1057280 | tf_op jit(solution)/shard_map/convert_element_type | solution.py:23
  4.8 0.8 fusion.4.x_ref
  5.7 114.0 %shard_map.91 = bf16[128,2048]{1,0:T(8,128)(2,1)} custom-call(bf16[128,2176]{1,0:T(8,128)(2,1)} %fusion.4.x_ref, bf16[2,2048,768]{2,1,0:T(8,128)(2,1)} %bitcast.3, bf16[2,768]{1,0:T(2,128)(2,1)} %bitcast.5, bf16[768,2048]{1,0:T(8,128)(2,1)} %bitcast.4, bf16[1,2048]{1,0:T(2,128)(2,1)} %down_scale_ref.1), custom_call_target="tpu_custom_call" | custom-call | flops 19327352832 | bytes 16777216 | tf_op jit(solution)/shard_map/pallas_call | solution.py:252
  119.7 1.9 %copy.17 = bf16[128,2048]{1,0:T(8,128)(2,1)} copy(bf16[128,2048]{1,0:T(8,128)(2,1)} %shard_map.91) | data formatting | bytes 1048576
  (4 shorter events, 0.0 us)

commit v3 on v2

--- a/solution.py
+++ b/solution.py
@@ -59,8 +59,8 @@
 
 
 def ring_kernel(
-    chips, experts, x_ref, in_ref, in_scale_ref, down_ref, down_scale_ref, out_ref,
-    rows, part, sib_in, ring_out, ring_in,
+    chips, experts, x_ref, in_hbm, in_scale_ref, down_hbm, down_scale_ref, out_ref,
+    in_ref, down_ref, load_sem, rows, part, sib_in, ring_out, ring_in,
     right_send, right_recv, left_send, left_recv, sib_send, sib_recv,
     give_send, give_recv, sum_send, sum_recv,
 ):
@@ -106,6 +106,12 @@
             part.at[block, 1 - core], sib_in.at[block], give_send.at[offset], give_recv.at[offset], sibling
         )
 
+    loads = (
+        pltpu.make_async_copy(in_hbm, in_ref, load_sem.at[0]),
+        pltpu.make_async_copy(down_hbm, down_ref, load_sem.at[1]),
+    )
+    for load in loads:
+        load.start()
     rows[chip, core] = x_ref[...]
     barrier = pltpu.get_barrier_semaphore()
     for target in (left, right, sibling):
@@ -118,6 +124,33 @@
     go_right(0, place).start()
     go_left(0, place).start()
     share(0, core).start()
+    for load in loads:
+        load.wait()
+
+    def sum_copy(way, step):
+        target = right if way == 0 else left
+        return remote(
+            ring_out.at[way, step], ring_in.at[way, step],
+            sum_send.at[way, step], sum_recv.at[way, step], target,
+        )
+
+    def own(offset, way):
+        block = chip_at(place + offset)
+        cut = slice(way * half, (way + 1) * half)
+        return part[block, core, :, cut].astype(jnp.float32) + sib_in[block, :, cut].astype(jnp.float32)
+
+    def sum_step(step, carry):
+        for way in range(2):
+            offset = chips - 1 - step if way == 0 else 1 + step
+            @pl.when((step < far_left) | ((step == far_left) & (way == 0)))
+            def _():
+                give(offset).wait()
+
+            mine = own(offset, way)
+            sum_copy(way, step - 1).wait_recv()
+            ring_out[way, step] = (mine + ring_in[way, step - 1].astype(jnp.float32)).astype(jnp.bfloat16)
+            sum_copy(way, step).start()
+        return carry
 
     def gather_step(k, carry):
         back = lax.rem(chips - k, chips)
@@ -168,41 +201,25 @@
             give(offset).start()
             return inner
 
-        return lax.fori_loop(0, sides, serve, carry)
+        lax.fori_loop(0, sides, serve, 0)
+
+        @pl.when(k == 1)
+        def _():
+            for way, first in ((0, chips - 1), (1, 1)):
+                give(first).wait()
+                ring_out[way, 0] = own(first, way).astype(jnp.bfloat16)
+                sum_copy(way, 0).start()
+
+        @pl.when(k >= 2)
+        def _():
+            sum_step(k - 1, 0)
+
+        return carry
 
     lax.fori_loop(0, far_right + 1, gather_step, 0)
 
-    def sum_copy(way, step):
-        target = right if way == 0 else left
-        return remote(
-            ring_out.at[way, step], ring_in.at[way, step],
-            sum_send.at[way, step], sum_recv.at[way, step], target,
-        )
-
-    def own(offset, way):
-        block = chip_at(place + offset)
-        cut = slice(way * half, (way + 1) * half)
-        return part[block, core, :, cut].astype(jnp.float32) + sib_in[block, :, cut].astype(jnp.float32)
-
-    def take(offset, carry):
-        give(offset).wait()
-        return carry
-
-    lax.fori_loop(0, chips, take, 0)
-    for way, first in ((0, chips - 1), (1, 1)):
-        ring_out[way, 0] = own(first, way).astype(jnp.bfloat16)
-        sum_copy(way, 0).start()
-
-    def sum_step(step, carry):
-        for way in range(2):
-            offset = chips - 1 - step if way == 0 else 1 + step
-            mine = own(offset, way)
-            sum_copy(way, step - 1).wait_recv()
-            ring_out[way, step] = (mine + ring_in[way, step - 1].astype(jnp.float32)).astype(jnp.bfloat16)
-            sum_copy(way, step).start()
-        return carry
-
-    lax.fori_loop(1, chips - 1, sum_step, 0)
+    lax.fori_loop(far_right, chips - 1, sum_step, 0)
+    give(0).wait()
     for way in range(2):
         mine = own(0, way)
         sum_copy(way, chips - 2).wait_recv()
@@ -252,9 +269,12 @@
     return pl.pallas_call(
         functools.partial(ring_kernel, chips, experts),
         out_shape=jax.ShapeDtypeStruct((tok_rows, model), jnp.bfloat16),
-        in_specs=[vmem] * 5,
+        in_specs=[vmem, pl.BlockSpec(memory_space=pl.ANY), vmem, pl.BlockSpec(memory_space=pl.ANY), vmem],
         out_specs=vmem,
         scratch_shapes=[
+            pltpu.VMEM(in_q.shape[1:], in_q.dtype),
+            pltpu.VMEM(down_q.shape[1:], down_q.dtype),
+            dma((2,)),
             pltpu.VMEM((chips, 2, tok_rows, width), jnp.bfloat16),
             pltpu.VMEM((chips, 2, tok_rows, model), jnp.bfloat16),
             pltpu.VMEM((chips, tok_rows, model), jnp.bfloat16),

time: 122 us -> 112 us (0.918)
  Pallas kernels: 114 us -> 104 us
    pallas_call x1, Pallas kernels: 114 us -> 104 us  [gathered(): pl.pallas_call(functools.partial(ring_kernel, chips, experts), out_shape=...]
where the time goes in v3:
time: 112 us
  Pallas kernels  104 us (93%)
  other arithmetic  5.53 us (5%)
  local copies, waits for them, and re-layouts  2 us (2%)
    pallas_call x1, Pallas kernels, gathered(): pl.pallas_call(functools.partial(ring_kernel, chips, experts), out_shape=...  104 us

profile of v3, /device:TPU:0, one launch (start us, length us, event | category | flops | bytes accessed | tf_op | source)
XLA Modules:
  0.0 111.6 jit_solution(205525583843660292)
XLA Ops:
  0.0 1.2 %fusion.1 = f32[128]{0:T(128)S(1)} fusion(bf16[128,2048]{1,0:T(8,128)(2,1)} %param.9), kind=kLoop, calls=%fused_computation.4 | loop fusion | flops 786304 | bytes 524800 | tf_op jit(solution)/shard_map/reduce_sum | solution.py:22
  1.2 0.7 reduce_sum.38
  1.9 0.7 broadcast_divide_fusion
  2.6 0.8 select_reduce_fusion.1
  3.5 0.1 copy.15
  3.6 1.2 %fusion.3 = bf16[128,2048]{1,0:T(8,128)(2,1)S(1)} fusion(bf16[128,2048]{1,0:T(8,128)(2,1)} %param.9, f32[2048]{0:T(1024)} %param.10, f32[128]{0:T(128)S(1)} %add_rsqrt_fusion), kind=kLoop, calls=%fused_computation.6 | loop fusion | flops 1048576 | bytes 1057280 | tf_op jit(solution)/shard_map/convert_element_type | solution.py:23
  4.8 0.8 fusion.4.x_ref
  5.7 104.0 %shard_map.91 = bf16[128,2048]{1,0:T(8,128)(2,1)} custom-call(bf16[128,2176]{1,0:T(8,128)(2,1)} %fusion.4.x_ref, bf16[2,2048,768]{2,1,0:T(8,128)(2,1)} %bitcast.3, bf16[2,768]{1,0:T(2,128)(2,1)} %bitcast.5, bf16[768,2048]{1,0:T(8,128)(2,1)} %bitcast.4, bf16[1,2048]{1,0:T(2,128)(2,1)} %down_scale_ref.1), custom_call_target="tpu_custom_call" | custom-call | flops 19327352832 | bytes 16777216 | tf_op jit(solution)/shard_map/pallas_call | solution.py:269
  109.7 1.9 %copy.17 = bf16[128,2048]{1,0:T(8,128)(2,1)} copy(bf16[128,2048]{1,0:T(8,128)(2,1)} %shard_map.91) | data formatting | bytes 1048576
  (4 shorter events, 0.0 us)

commit v4 on v3

--- a/solution.py
+++ b/solution.py
@@ -66,7 +66,8 @@
 ):
     depth = chips // 2
     model = out_ref.shape[1]
-    half = model // 2
+    ways = ring_out.shape[0]
+    wide = model // ways
     me = lax.axis_index("tok")
     core = lax.rem(me, 2)
     chip = me // 2
@@ -128,7 +129,7 @@
         load.wait()
 
     def sum_copy(way, step):
-        target = right if way == 0 else left
+        target = right if way % 2 == 0 else left
         return remote(
             ring_out.at[way, step], ring_in.at[way, step],
             sum_send.at[way, step], sum_recv.at[way, step], target,
@@ -136,15 +137,16 @@
 
     def own(offset, way):
         block = chip_at(place + offset)
-        cut = slice(way * half, (way + 1) * half)
+        cut = slice(way * wide, (way + 1) * wide)
         return part[block, core, :, cut].astype(jnp.float32) + sib_in[block, :, cut].astype(jnp.float32)
 
     def sum_step(step, carry):
-        for way in range(2):
-            offset = chips - 1 - step if way == 0 else 1 + step
-            @pl.when((step < far_left) | ((step == far_left) & (way == 0)))
-            def _():
-                give(offset).wait()
+        for way in range(ways):
+            offset = chips - 1 - step if way % 2 == 0 else 1 + step
+            if way < 2:
+                @pl.when((step < far_left) | ((step == far_left) & (way == 0)))
+                def _():
+                    give(offset).wait()
 
             mine = own(offset, way)
             sum_copy(way, step - 1).wait_recv()
@@ -192,12 +194,12 @@
             up = jnp.dot(values, in_ref[1], preferred_element_type=jnp.float32)
             up = up * in_scale_ref[1:2, :].astype(jnp.float32)
             hidden = (gate / (1.0 + jnp.exp(-gate)) * up).astype(jnp.bfloat16)
-            wide = model // 4
+            run = model // 4
             for piece in range(4):
-                cut = slice(piece * wide, (piece + 1) * wide)
+                cut = slice(piece * run, (piece + 1) * run)
                 served = jnp.dot(hidden, down_ref[:, cut], preferred_element_type=jnp.float32)
                 served = served * down_scale_ref[:, cut].astype(jnp.float32) * weight
-                part[block, :, :, cut] = served.astype(jnp.bfloat16).reshape(2, -1, wide)
+                part[block, :, :, cut] = served.astype(jnp.bfloat16).reshape(2, -1, run)
             give(offset).start()
             return inner
 
@@ -205,8 +207,10 @@
 
         @pl.when(k == 1)
         def _():
-            for way, first in ((0, chips - 1), (1, 1)):
-                give(first).wait()
+            give(chips - 1).wait()
+            give(1).wait()
+            for way in range(ways):
+                first = chips - 1 if way % 2 == 0 else 1
                 ring_out[way, 0] = own(first, way).astype(jnp.bfloat16)
                 sum_copy(way, 0).start()
 
@@ -220,15 +224,15 @@
 
     lax.fori_loop(far_right, chips - 1, sum_step, 0)
     give(0).wait()
-    for way in range(2):
+    for way in range(ways):
         mine = own(0, way)
         sum_copy(way, chips - 2).wait_recv()
         total = mine + ring_in[way, chips - 2].astype(jnp.float32)
-        out_ref[:, way * half : (way + 1) * half] = total.astype(jnp.bfloat16)
+        out_ref[:, way * wide : (way + 1) * wide] = total.astype(jnp.bfloat16)
 
     def ended(step, carry):
-        sum_copy(0, step).wait_send()
-        sum_copy(1, step).wait_send()
+        for way in range(ways):
+            sum_copy(way, step).wait_send()
         return carry
 
     lax.fori_loop(0, chips - 1, ended, 0)
@@ -265,7 +269,7 @@
     vmem = pl.BlockSpec(memory_space=pltpu.VMEM)
     dma = pltpu.SemaphoreType.DMA
     total_rows = 2 * chips * tok_rows
-    half = model // 2
+    ways = 4
     return pl.pallas_call(
         functools.partial(ring_kernel, chips, experts),
         out_shape=jax.ShapeDtypeStruct((tok_rows, model), jnp.bfloat16),
@@ -278,10 +282,10 @@
             pltpu.VMEM((chips, 2, tok_rows, width), jnp.bfloat16),
             pltpu.VMEM((chips, 2, tok_rows, model), jnp.bfloat16),
             pltpu.VMEM((chips, tok_rows, model), jnp.bfloat16),
-            pltpu.VMEM((2, chips - 1, tok_rows, half), jnp.bfloat16),
-            pltpu.VMEM((2, chips - 1, tok_rows, half), jnp.bfloat16),
+            pltpu.VMEM((ways, chips - 1, tok_rows, model // ways), jnp.bfloat16),
+            pltpu.VMEM((ways, chips - 1, tok_rows, model // ways), jnp.bfloat16),
             dma((chips,)), dma((chips,)), dma((chips,)), dma((chips,)), dma((chips,)), dma((chips,)),
-            dma((chips,)), dma((chips,)), dma((2, chips - 1)), dma((2, chips - 1)),
+            dma((chips,)), dma((chips,)), dma((ways, chips - 1)), dma((ways, chips - 1)),
         ],
         compiler_params=pltpu.CompilerParams(
             collective_id=0, has_side_effects=True, vmem_limit_bytes=60 * 1024 * 1024

time: 112 us -> 109 us (0.973)
  Pallas kernels: 104 us -> 101 us
    pallas_call x1, Pallas kernels: 104 us -> 101 us  [gathered(): pl.pallas_call(functools.partial(ring_kernel, chips, experts), out_shape=...]
where the time goes in v4:
time: 109 us
  Pallas kernels  101 us (93%)
  other arithmetic  5.53 us (5%)
  local copies, waits for them, and re-layouts  2 us (2%)
    pallas_call x1, Pallas kernels, gathered(): pl.pallas_call(functools.partial(ring_kernel, chips, experts), out_shape=...  101 us

profile of v4, /device:TPU:0, one launch (start us, length us, event | category | flops | bytes accessed | tf_op | source)
XLA Modules:
  0.0 109.0 jit_solution(12447775174694294912)
XLA Ops:
  0.0 1.2 %fusion.1 = f32[128]{0:T(128)S(1)} fusion(bf16[128,2048]{1,0:T(8,128)(2,1)} %param.9), kind=kLoop, calls=%fused_computation.4 | loop fusion | flops 786304 | bytes 524800 | tf_op jit(solution)/shard_map/reduce_sum | solution.py:22
  1.2 0.7 reduce_sum.38
  1.9 0.7 broadcast_divide_fusion
  2.6 0.8 select_reduce_fusion.1
  3.5 0.1 copy.15
  3.6 1.2 %fusion.3 = bf16[128,2048]{1,0:T(8,128)(2,1)S(1)} fusion(bf16[128,2048]{1,0:T(8,128)(2,1)} %param.9, f32[2048]{0:T(1024)} %param.10, f32[128]{0:T(128)S(1)} %add_rsqrt_fusion), kind=kLoop, calls=%fused_computation.6 | loop fusion | flops 1048576 | bytes 1057280 | tf_op jit(solution)/shard_map/convert_element_type | solution.py:23
  4.8 0.8 fusion.4.x_ref
  5.7 101.4 %shard_map.91 = bf16[128,2048]{1,0:T(8,128)(2,1)} custom-call(bf16[128,2176]{1,0:T(8,128)(2,1)} %fusion.4.x_ref, bf16[2,2048,768]{2,1,0:T(8,128)(2,1)} %bitcast.3, bf16[2,768]{1,0:T(2,128)(2,1)} %bitcast.5, bf16[768,2048]{1,0:T(8,128)(2,1)} %bitcast.4, bf16[1,2048]{1,0:T(2,128)(2,1)} %down_scale_ref.1), custom_call_target="tpu_custom_call" | custom-call | flops 19327352832 | bytes 16777216 | tf_op jit(solution)/shard_map/pallas_call | solution.py:273
  107.1 1.9 %copy.17 = bf16[128,2048]{1,0:T(8,128)(2,1)} copy(bf16[128,2048]{1,0:T(8,128)(2,1)} %shard_map.91) | data formatting | bytes 1048576
  (4 shorter events, 0.0 us)

commit v5 on v4

--- a/solution.py
+++ b/solution.py
@@ -59,7 +59,7 @@
 
 
 def ring_kernel(
-    chips, experts, x_ref, in_hbm, in_scale_ref, down_hbm, down_scale_ref, out_ref,
+    chips, experts, x_ref, gain_ref, ids_ref, gates_ref, owner_ref, in_hbm, in_scale_ref, down_hbm, down_scale_ref, out_ref,
     in_ref, down_ref, load_sem, rows, part, sib_in, ring_out, ring_in,
     right_send, right_recv, left_send, left_recv, sib_send, sib_recv,
     give_send, give_recv, sum_send, sum_recv,
@@ -98,6 +98,20 @@
     def go_left(k, position):
         return row_copy(position, core, left_send.at[k], left_recv.at[k], left)
 
+    far_right, far_left = chips // 2, chips - 1 - chips // 2
+    tok_half = x_ref.shape[0] // 2
+
+    def far_rows(position, low):
+        return rows.at[chip_at(position), core, low * tok_half : (low + 1) * tok_half]
+
+    def end_right(position):
+        block = far_rows(position, 0)
+        return remote(block, block, right_send.at[far_right - 1], right_recv.at[far_right - 1], right)
+
+    def end_left(position):
+        block = far_rows(position, 1)
+        return remote(block, block, left_send.at[far_left], left_recv.at[far_left], left)
+
     def share(offset, side):
         return row_copy(place + offset, side, sib_send.at[offset], sib_recv.at[offset], sibling)
 
@@ -113,15 +127,32 @@
     )
     for load in loads:
         load.start()
-    rows[chip, core] = x_ref[...]
     barrier = pltpu.get_barrier_semaphore()
     for target in (left, right, sibling):
         pl.semaphore_signal(
             barrier, inc=1, device_id={"tok": target}, device_id_type=pl.DeviceIdType.MESH
         )
+
+    values = x_ref[...].astype(jnp.float32)
+    row_scale = lax.rsqrt(jnp.mean(values * values, axis=1, keepdims=True) + 1e-06)
+    rows[chip, core, :, :model] = (values * row_scale * gain_ref[...]).astype(jnp.bfloat16)
+    weights = gates_ref[...] / jnp.sum(gates_ref[...], axis=1, keepdims=True)
+    lane = lax.broadcasted_iota(jnp.int32, (x_ref.shape[0], rows.shape[3] - model), 1)
+    named = jnp.full(lane.shape, -1, jnp.int32)
+    for expert in range(experts):
+        slot = owner_ref[expert]
+        served_there = (lane == slot) | (lane == slot + experts) | (lane == slot + 2 * experts)
+        named = jnp.where(served_there, expert, named)
+    shares = jnp.zeros(lane.shape, jnp.float32)
+    for k in range(ids_ref.shape[1]):
+        shares += jnp.where(ids_ref[:, k : k + 1] == named, weights[:, k : k + 1], 0.0)
+    high = shares.astype(jnp.bfloat16).astype(jnp.float32)
+    middle = (shares - high).astype(jnp.bfloat16).astype(jnp.float32)
+    low = shares - high - middle
+    split = jnp.where(lane < experts, high, jnp.where(lane < 2 * experts, middle, low))
+    rows[chip, core, :, model:] = split.astype(jnp.bfloat16)
     pl.semaphore_wait(barrier, 3)
 
-    far_right, far_left = chips // 2, chips - 1 - chips // 2
     go_right(0, place).start()
     go_left(0, place).start()
     share(0, core).start()
@@ -157,25 +188,36 @@
     def gather_step(k, carry):
         back = lax.rem(chips - k, chips)
 
-        @pl.when(k >= 1)
+        @pl.when((k >= 1) & (k <= far_left))
         def _():
             go_right(k - 1, place - k).wait_recv()
 
-            @pl.when(k < far_right)
+            @pl.when(k < far_left)
             def _():
                 go_right(k, place - k).start()
 
+            @pl.when(k == far_left)
+            def _():
+                end_right(place - k).start()
+
             share(back, core).start()
-
-        @pl.when((k >= 1) & (k <= far_left))
-        def _():
             go_left(k - 1, place + k).wait_recv()
 
             @pl.when(k < far_left)
             def _():
                 go_left(k, place + k).start()
 
+            @pl.when(k == far_left)
+            def _():
+                end_left(place + k).start()
+
             share(k, core).start()
+
+        @pl.when(k == far_right)
+        def _():
+            end_right(place - k).wait_recv()
+            end_left(place + k).wait_recv()
+            share(back, core).start()
 
         sides = jnp.where((k >= 1) & (k <= far_left), 2, 1)
 
@@ -242,10 +284,11 @@
         return carry
 
     lax.fori_loop(0, chips, shared, 0)
-    for k in range(far_right):
+    for k in range(far_left):
         go_right(k, place - k).wait_send()
-    for k in range(far_left):
         go_left(k, place + k).wait_send()
+    end_right(place - far_left).wait_send()
+    end_left(place + far_left).wait_send()
 
 
 def gathered(
@@ -254,18 +297,7 @@
     experts = owner_map.shape[0]
     tok_rows, model = tokens.shape
     chips = experts // 2
-    normed = normalised(tokens, norm_gain)
-    weights = gate_weights / jnp.sum(gate_weights, axis=1, keepdims=True)
-    labels = jnp.arange(experts, dtype=jnp.int32)
-    slot_table = jnp.sum(jnp.where(expert_ids[:, :, None] == labels, owner_map, 0), axis=2)
-    shares = jnp.sum(jnp.where(slot_table[:, :, None] == labels, weights[:, :, None], 0.0), axis=1)
-    high = lax.reduce_precision(shares, 8, 7)
-    middle = lax.reduce_precision(shares - high, 8, 7)
-    low = shares - high - middle
-    lanes = jnp.concatenate([high, middle, low], axis=1).astype(jnp.bfloat16)
-    pad = -lanes.shape[1] % 128
-    rows = jnp.concatenate([normed, jnp.pad(lanes, ((0, 0), (0, pad)))], axis=1)
-    width = rows.shape[1]
+    width = model + 128 * ((3 * experts + 127) // 128)
     vmem = pl.BlockSpec(memory_space=pltpu.VMEM)
     dma = pltpu.SemaphoreType.DMA
     total_rows = 2 * chips * tok_rows
@@ -273,7 +305,7 @@
     return pl.pallas_call(
         functools.partial(ring_kernel, chips, experts),
         out_shape=jax.ShapeDtypeStruct((tok_rows, model), jnp.bfloat16),
-        in_specs=[vmem, pl.BlockSpec(memory_space=pl.ANY), vmem, pl.BlockSpec(memory_space=pl.ANY), vmem],
+        in_specs=[vmem] * 4 + [pl.BlockSpec(memory_space=pltpu.SMEM), pl.BlockSpec(memory_space=pl.ANY), vmem, pl.BlockSpec(memory_space=pl.ANY), vmem],
         out_specs=vmem,
         scratch_shapes=[
             pltpu.VMEM(in_q.shape[1:], in_q.dtype),
@@ -293,7 +325,7 @@
         cost_estimate=pl.CostEstimate(
             flops=6 * total_rows * model * in_q.shape[3], bytes_accessed=4 * total_rows * model, transcendentals=0
         ),
-    )(rows, in_q[0], in_scale[0], down_q[0], down_scale)
+    )(tokens, norm_gain[None, :], expert_ids, gate_weights, owner_map, in_q[0], in_scale[0], down_q[0], down_scale)
 
 
 def solution(mesh):
@@ -312,7 +344,7 @@
 
     def on_device(*args):
         experts, top_count = args[4].shape[0], args[2].shape[1]
-        body = gathered if experts <= 2 * top_count and experts % 4 == 0 else dispatched
+        body = gathered if experts <= 2 * top_count and experts % 8 == 0 else dispatched
         return body(*args)
 
     return jax.shard_map(

time: 109 us -> 99.3 us (0.911)
  Pallas kernels: 101 us -> 94.4 us
  other arithmetic: 5.53 us -> 0 us
  local copies, waits for them, and re-layouts: 2 us -> 4.7 us
    pallas_call x1, Pallas kernels: 101 us -> 94.4 us  [gathered(): pl.pallas_call(functools.partial(ring_kernel, chips, experts), out_shape=...]
    unnamed x1 -> x3, local copies, waits for them, and re-layouts: 1.88 us -> 4.7 us
    reduce_sum x4 -> x0, other arithmetic: 2.74 us -> none  [the longest x1 1.23 us: normalised(): jnp.mean(values * values, axis=1, keepdims=True) + 1e-06]
    convert_element_type x1 -> x0, other arithmetic: 1.24 us -> none  [normalised(): return (values * row_scale * norm_gain).astype(jnp.bfloat16)]
where the time goes in v5:
time: 99.3 us; the launch traced here: 99.1 us
  Pallas kernels  94.4 us (95%)
  local copies, waits for them, and re-layouts  4.7 us (5%)
    pallas_call x1, Pallas kernels, gathered(): pl.pallas_call(functools.partial(ring_kernel, chips, experts), out_shape=...  94.4 us
    unnamed x3, local copies, waits for them, and re-layouts  4.7 us

profile of v5, /device:TPU:0, one launch (start us, length us, event | category | flops | bytes accessed | tf_op | source)
XLA Modules:
  0.0 99.1 jit_solution(13210394128479146843)
XLA Ops:
  0.0 1.4 %copy.10.ids_ref = s32[128,8]{1,0:T(8,128)} copy(s32[128,8]{0,1:T(8,128)} %param.11) | data formatting | bytes 8192 | tf_op args[2]
  1.4 1.4 %copy.11.gates_ref = f32[128,8]{1,0:T(8,128)} copy(f32[128,8]{0,1:T(8,128)} %param.12) | data formatting | bytes 8192 | tf_op args[3]
  2.8 94.4 %shard_map.91 = bf16[128,2048]{1,0:T(8,128)(2,1)} custom-call(bf16[128,2048]{1,0:T(8,128)(2,1)} %x_ref.1, f32[1,2048]{1,0:T(1,128)} %bitcast.6, s32[128,8]{1,0:T(8,128)} %copy.10.ids_ref, f32[128,8]{1,0:T(8,128)} %copy.11.gates_ref, s32[16]{0:T(128)} %owner_ref.1, bf16[2,2048,768]{2,1,0:T(8,128)(2,1)} %bitcast.4, bf16[2,768]{1,0:T(2,128)(2,1)} %bitcast.7, ...), custom_call_target="tpu_custom_call" | custom-call | flops 19327352832 | bytes 16777216 | tf_op jit(solution)/shard_map/pallas_call | solution.py:305
  97.2 1.9 %copy.13 = bf16[128,2048]{1,0:T(8,128)(2,1)} copy(bf16[128,2048]{1,0:T(8,128)(2,1)} %shard_map.91) | data formatting | bytes 1048576
